TPU v7x, 128 devices: a whole 4x4x4 slice. The times are simulated.
128 devices in a mesh: band: 8 (over z_lo, y), fft: 16 (over x, z_hi, core).
Axes of the slice: x: 4, y: 4, z: 4 (z_hi: 2, z_lo: 2; z = z_hi * 2 + z_lo), core: 2. Of those that a mesh axis runs over, the one named last changes fastest.
Arguments:
- orbitals: float32 [8, 256, 256, 256], P('band', 'fft'), may hold values from -6 to 6
- pair_flags: int32 [8, 2], replicated, may hold values 0 or 1
- cutoff_reach: int32 [129, 129], replicated, may hold values from 0 to 128
Outputs:
- exchange_field: float32 [8, 256, 256, 256], P('band', 'fft')
- margin: float32 [8, 1], P('band')
All inputs are finite; a program needn't handle non-finite values.
Results may differ from a plain program's by a relative error of at most 0.0003.
Values sent between devices are 32-bit elements; how exact they have to be, the bound alone decides.
A program may use at most 128 MiB of HBM per device.

v0:
```python
import math

import jax
import jax.numpy as jnp
from jax import lax
from jax.sharding import PartitionSpec as P

highest = lax.Precision.HIGHEST


def from_behind(block, axis, distance):
    devices = range(lax.axis_size(axis))
    route = [((i - distance) % len(devices), i) for i in devices]
    return lax.ppermute(block, axis, route)


def cas_matrix(grid_size):
    indices = jnp.arange(grid_size, dtype=jnp.int32)
    phases = indices[:, None] * indices[None, :] % grid_size
    angles = phases.astype(jnp.float32) * (2.0 * math.pi / grid_size)
    return jnp.cos(angles) + jnp.sin(angles)


def folded(grid_size):
    indices = jnp.arange(grid_size, dtype=jnp.int32)
    return jnp.minimum(indices, grid_size - indices)


def kernel_block(cutoff_reach, grid_size, first_row, y_width):
    fold_all = folded(grid_size)
    levels = jnp.arange(cutoff_reach.shape[0], dtype=jnp.int32)
    pick_x = (fold_all[:, None] == levels[None, :]).astype(jnp.float32)
    fold_y = lax.dynamic_slice_in_dim(fold_all, first_row, y_width)
    pick_y = (fold_y[:, None] == levels[None, :]).astype(jnp.float32)
    reach_map = jnp.dot(
        jnp.dot(pick_x, cutoff_reach.astype(jnp.float32), precision=highest),
        pick_y.T,
        precision=highest,
    )
    inside = fold_all.astype(jnp.float32)[None, None, :] <= reach_map[:, :, None]
    squares = (
        fold_all[:, None, None] * fold_all[:, None, None]
        + fold_y[None, :, None] * fold_y[None, :, None]
        + fold_all[None, None, :] * fold_all[None, None, :]
    )
    safe_sq = jnp.maximum(squares, 1).astype(jnp.float32)
    return jnp.where(inside & (squares > 0), 64.0 / safe_sq, 0.0) / float(
        grid_size * grid_size * grid_size
    )


def transform_inner(densities, cas_table):
    along_z = jnp.einsum("pxyz,zk->pxyk", densities, cas_table, precision=highest)
    return jnp.einsum("pxyz,yk->pxkz", along_z, cas_table, precision=highest)


def on_device(orbitals, pair_flags, cutoff_reach):
    grid_size = orbitals.shape[2]
    band_count = orbitals.shape[0]
    cas_table = cas_matrix(grid_size)
    cycle_size = lax.axis_size("band")
    position = lax.axis_index("band")
    weights = pair_flags.astype(jnp.float32)
    own_weight = weights[position, 0]
    next_weight = weights[position, 1]
    prev_weight = weights[(position + cycle_size - 1) % cycle_size, 1]
    own_pairs = [(a, b) for a in range(band_count) for b in range(a, band_count)]
    cross_pairs = [(a, b) for a in range(band_count) for b in range(band_count)]
    terms = [own_weight * orbitals[a] * orbitals[b] for a, b in own_pairs]
    following = from_behind(orbitals, "band", -1)
    terms = terms + [next_weight * orbitals[a] * following[b] for a, b in cross_pairs]
    preceding = from_behind(orbitals, "band", 1)
    terms = terms + [prev_weight * preceding[b] * orbitals[a] for a, b in cross_pairs]
    spectrum = transform_inner(jnp.stack(terms), cas_table)
    y_width = grid_size // lax.axis_size("fft")
    kernel = kernel_block(cutoff_reach, grid_size, lax.axis_index("fft") * y_width, y_width)
    along_x = jnp.einsum(
        "pxyz,xk->pkyz",
        lax.all_to_all(spectrum, "fft", split_axis=2, concat_axis=1, tiled=True),
        cas_table,
        precision=highest,
    )
    scaled = along_x * kernel[None]
    restored = jnp.einsum("pxyz,xk->pkyz", scaled, cas_table, precision=highest)
    mixed = lax.all_to_all(restored, "fft", split_axis=1, concat_axis=2, tiled=True)
    potentials = transform_inner(mixed, cas_table)
    applied = [jnp.zeros(orbitals.shape[1:], jnp.float32)]
    cursor = 0
    a, b = own_pairs[0]
    coulomb = potentials[cursor]
    cursor = cursor + 1
    applied[a] = applied[a] - orbitals[b] * coulomb
    handed = [jnp.zeros(orbitals.shape[1:], jnp.float32)]
    a, b = cross_pairs[0]
    coulomb = potentials[cursor]
    cursor = cursor + 1
    applied[a] = applied[a] - following[b] * coulomb
    handed[b] = handed[b] - orbitals[a] * coulomb
    a, b = cross_pairs[0]
    coulomb = potentials[cursor]
    applied[a] = applied[a] - preceding[b] * coulomb
    applied_all = jnp.stack(applied)
    local_margin = jnp.einsum("axyz,bxyz->ab", orbitals, applied_all, precision=highest)
    margin = lax.psum(local_margin, "fft") / float(grid_size * grid_size)
    return (applied_all, margin)


def solution(mesh):
    return jax.shard_map(
        on_device,
        mesh=mesh,
        in_specs=(P("band", "fft", None, None), P(), P()),
        out_specs=(P("band", "fft", None, None), P("band", None)),
        check_vma=False,
    )
```

profile of v0, /device:TPU:1, one launch (start us, length us, event | category | flops | bytes accessed | tf_op | source)
XLA Modules:
  0.0 676.7 jit_solution(113064284837226663)
XLA Ops:
  0.6 5.0 collective-permute-start
  5.6 0.0 collective-permute-start.1
  5.6 0.7 convert_element_type.36
  6.3 0.6 constant_dynamic-slice_fusion.2
  6.9 88.3 %collective-permute-done = f32[1,16,256,256]{3,2,1,0:T(8,128)} collective-permute-done((f32[1,16,256,256]{3,2,1,0:T(8,128)}, f32[1,16,256,256]{3,2,1,0:T(8,128)}, u32[]{:S(2)}, u32[]{:S(2)}) %collective-permute-start) | collective-permute-done | bytes 4194336 | tf_op jit(solution)/shard_map/ppermute | solution.py:14
  95.2 4.0 collective-permute-done.1
  99.2 11.5 %multiply_multiply_fusion = (f32[1,16,256,256]{3,2,1,0:T(8,128)S(1)}, f32[1,16,256,256]{3,2,1,0:T(8,128)}, f32[1,16,256,256]{3,2,1,0:T(8,128)}) fusion(f32[1,16,256,256]{3,2,1,0:T(8,128)} %param.3, f32[]{:T(128)} %bitcast.3, f32[1,16,256,256]{3,2,1,0:T(8,128)} %collective-permute-done, f32[]{:T(128)} %bitcast.4, ...), kind=kLoop, calls=%fused_computation.12 | loop fusion | flops 6291456 | bytes 25165836 | tf_op jit(solution)/shard_map/mul | solution.py:69
  110.6 14.5 %fusion = f32[3,16,256,256]{3,2,1,0:T(8,128)S(1)} fusion(f32[1,16,256,256]{3,2,1,0:T(8,128)} %get-tuple-element.8, f32[1,16,256,256]{3,2,1,0:T(8,128)} %get-tuple-element.7, f32[1,16,256,256]{3,2,1,0:T(8,128)S(1)} %get-tuple-element.6), kind=kOutput, calls=%fused_computation | convolution fusion | flops 9670950912 | bytes 25165824 | tf_op jit(solution)/shard_map/pxyz,zk->pxyk/dot_general | solution.py:53
  125.1 16.6 %convolution_bitcast_fusion.1 = f32[3,16,256,256]{3,2,1,0:T(8,128)} fusion(f32[3,16,256,256]{3,2,1,0:T(8,128)S(1)} %fusion), kind=kOutput, calls=%fused_computation.17 | convolution fusion | flops 9664659456 | bytes 25165824 | tf_op jit(solution)/shard_map/pxyz,yk->pxkz/dot_general | solution.py:54
  141.7 16.3 %copy.13 = f32[3,16,256,256]{3,1,0,2:T(8,128)} copy(f32[3,16,256,256]{3,2,1,0:T(8,128)} %convolution_bitcast_fusion.1) | data formatting | bytes 25165824 | tf_op jit(solution)/shard_map/pxyz,yk->pxkz/transpose | solution.py:54
  158.1 0.0 copy-start.1
  158.1 9.3 %all-to-all-start = ((f32[3,16,256,256]{3,1,0,2:T(8,128)}), f32[3,16,256,256]{3,1,0,2:T(8,128)}, u32[]{:S(2)}, u32[]{:S(2)}) async-start(f32[3,16,256,256]{3,1,0,2:T(8,128)} %copy.13), calls=%async_computation | async-start | bytes 25165824 | tf_op jit(solution)/shard_map/all_to_all | solution.py:79
  167.4 0.1 fusion.70
  167.5 0.1 broadcast_add_fusion
  167.6 0.0 copy-done.1
  167.6 0.4 fusion.37
  168.0 0.2 fusion.40
  168.1 3.7 fusion.18
  171.8 195.7 %all-to-all-done = f32[3,16,256,256]{3,1,0,2:T(8,128)} async-done(((f32[3,16,256,256]{3,1,0,2:T(8,128)}), f32[3,16,256,256]{3,1,0,2:T(8,128)}, u32[]{:S(2)}, u32[]{:S(2)}) %all-to-all-start) | async-done | bytes 12582944 | tf_op jit(solution)/shard_map/all_to_all | solution.py:79
  367.6 21.1 %copy.15 = f32[3,16,16,16,256]{4,3,2,1,0:T(8,128)} copy(f32[3,16,16,16,256]{4,2,0,3,1:T(8,128)} %bitcast.10) | data formatting | bytes 25165824 | tf_op jit(solution)/shard_map/all_to_all | solution.py:79
  388.7 0.0 copy-start
  388.7 21.7 %fusion.8 = f32[256,3,16,256]{3,0,2,1:T(8,128)S(1)} fusion(f32[3,256,16,256]{3,2,1,0:T(8,128)} %bitcast.50), kind=kOutput, calls=%fused_computation.8 | convolution fusion | flops 9664659456 | bytes 25165824 | tf_op jit(solution)/shard_map/pxyz,xk->pkyz/dot_general | solution.py:77
  410.4 0.0 copy-done
  410.4 16.8 %fusion.12 = f32[3,256,16,256]{3,1,2,0:T(8,128)} fusion(f32[256,3,16,256]{3,0,2,1:T(8,128)S(1)} %fusion.8, f32[256,16,256]{2,0,1:T(8,128)S(1)} %copy-done), kind=kOutput, calls=%fused_computation.15 | convolution fusion | flops 9667805184 | bytes 29360128 | tf_op jit(solution)/shard_map/pxyz,xk->pkyz/dot_general | solution.py:84
  427.3 16.4 %copy.17 = f32[3,256,16,256]{3,2,0,1:T(8,128)} copy(f32[3,256,16,256]{3,1,2,0:T(8,128)} %fusion.12) | data formatting | bytes 25165824 | tf_op jit(solution)/shard_map/pxyz,xk->pkyz/transpose | solution.py:84
  443.7 149.1 %all_to_all.36 = f32[3,256,16,256]{3,2,0,1:T(8,128)} all-to-all(f32[3,256,16,256]{3,2,0,1:T(8,128)} %copy.17), channel_id=1, replica_groups=mesh['band'=8,'fft'=16] {'fft'}, dimensions={1} | all-to-all | bytes 25165824 | tf_op jit(solution)/shard_map/all_to_all | solution.py:85
  592.8 11.4 %copy.19 = f32[3,16,16,16,256]{4,3,2,1,0:T(8,128)} copy(f32[3,16,16,16,256]{4,3,0,1,2:T(8,128)} %bitcast.51) | data formatting | bytes 25165824 | tf_op jit(solution)/shard_map/all_to_all | solution.py:85
  604.1 15.8 %fusion.27 = f32[3,16,256,256]{3,2,1,0:T(8,128)S(1)} fusion(f32[3,16,256,256]{3,2,1,0:T(8,128)} %bitcast.52), kind=kOutput, calls=%fused_computation.39 | convolution fusion | flops 9664659456 | bytes 25165824 | tf_op jit(solution)/shard_map/pxyz,zk->pxyk/dot_general | solution.py:53
  620.0 12.6 %convolution_bitcast_fusion = f32[3,16,256,256]{3,2,1,0:T(8,128)S(1)} fusion(f32[3,16,256,256]{3,2,1,0:T(8,128)S(1)} %fusion.27), kind=kOutput, calls=%fused_computation.16 | convolution fusion | flops 9664659456 | bytes 25165824 | tf_op jit(solution)/shard_map/pxyz,yk->pxkz/dot_general | solution.py:54
  632.6 7.6 %fusion.22 = (f32[]{:T(128)}, f32[1,16,256,256]{3,2,1,0:T(8,128)}) fusion(f32[1,16,256,256]{3,2,1,0:T(8,128)} %param.3, f32[1,16,256,256]{3,2,1,0:T(8,128)} %collective-permute-done.1, f32[3,16,256,256]{3,2,1,0:T(8,128)S(1)} %convolution_bitcast_fusion, f32[1,16,256,256]{3,2,1,0:T(8,128)} %collective-permute-done), kind=kLoop, calls=%fused_computation.29 | loop fusion | flops 8388607 | bytes 29360132 | tf_op jit(solution)/shard_map/axyz,bxyz->ab/dot_general | solution.py:103
  640.2 34.5 %psum.7 = f32[1,1]{1,0:T(1,128)} all-reduce(f32[1,1]{1,0:T(1,128)} %bitcast.22), channel_id=1, replica_groups=mesh['band'=8,'fft'=16] {'fft'}, use_global_device_ids=true, to_apply=%region_0.1 | all-reduce | flops 1 | bytes 8 | tf_op jit(solution)/shard_map/psum | solution.py:104
  (2 shorter events, 0.0 us)
Async XLA Ops:
  0.6 94.5 %collective-permute-start = (f32[1,16,256,256]{3,2,1,0:T(8,128)}, f32[1,16,256,256]{3,2,1,0:T(8,128)}, u32[]{:S(2)}, u32[]{:S(2)}) collective-permute-start(f32[1,16,256,256]{3,2,1,0:T(8,128)} %param.3), channel_id=1, source_target_pairs={{16,0},{32,16},{48,32},{64,48},{80,64},{96,80},{112,96},{0,112},{1... | collective-permute-start | bytes 12582920 | tf_op jit(solution)/shard_map/ppermute | solution.py:14
  5.6 93.5 %collective-permute-start.1 = (f32[1,16,256,256]{3,2,1,0:T(8,128)}, f32[1,16,256,256]{3,2,1,0:T(8,128)}, u32[]{:S(2)}, u32[]{:S(2)}) collective-permute-start(f32[1,16,256,256]{3,2,1,0:T(8,128)} %param.3), channel_id=1, source_target_pairs={{112,0},{0,16},{16,32},{32,48},{48,64},{64,80},{80,96},{96,112},{1... | collective-permute-start | bytes 12582920 | tf_op jit(solution)/shard_map/ppermute | solution.py:14
  158.1 9.5 %copy-start.1 = (s32[129,129]{1,0:T(8,128)S(1)}, s32[129,129]{1,0:T(8,128)}, u32[]{:S(2)}) copy-start(s32[129,129]{1,0:T(8,128)} %param.5) | copy-start | bytes 199696
  158.1 209.5 %all-to-all-start = ((f32[3,16,256,256]{3,1,0,2:T(8,128)}), f32[3,16,256,256]{3,1,0,2:T(8,128)}, u32[]{:S(2)}, u32[]{:S(2)}) async-start(f32[3,16,256,256]{3,1,0,2:T(8,128)} %copy.13), calls=%async_computation | async-start | bytes 25165824 | tf_op jit(solution)/shard_map/all_to_all | solution.py:79
  388.7 21.7 %copy-start = (f32[256,16,256]{2,0,1:T(8,128)S(1)}, f32[256,16,256]{2,0,1:T(8,128)}, u32[]{:S(2)}) copy-start(f32[256,16,256]{2,0,1:T(8,128)} %fusion.18) | copy-start | bytes 12582916
where the time goes:
time: 687 us; the launch traced here: 677 us
  waiting for transfers between devices  288 us (42%)
  blocking collectives  184 us (27%)
  matrix products  98.7 us (14%)
  local copies, waits for them, and re-layouts  65.8 us (10%)
  other arithmetic  23.6 us (3%)
  starting transfers between devices  14.3 us (2%)
    all_to_all x1, waiting for transfers between devices, on_device(): lax.all_to_all(spectrum, 'fft', split_axis=2, concat_axis=1, tiled=True)  196 us
    all_to_all x1, blocking collectives, on_device(): lax.all_to_all(restored, 'fft', split_axis=1, concat_axis=2, tiled=True)  149 us
    ppermute x2, waiting for transfers between devices, from_behind(): return lax.ppermute(block, axis, route)  92.2 us
    psum x1, blocking collectives, on_device(): margin = lax.psum(local_margin, 'fft') / float(grid_size * grid_size)  34.5 us
    dot_general x2, matrix products, transform_inner(): jnp.einsum('pxyz,zk->pxyk', densities, cas_table, precision=highest)  30.3 us
    dot_general x2, matrix products, transform_inner(): return jnp.einsum('pxyz,yk->pxkz', along_z, cas_table, precision=highest)  29.2 us
    dot_general x1, matrix products, on_device(): jnp.einsum('pxyz,xk->pkyz', lax.all_to_all(spectrum, 'fft', split_axis=2,...  21.7 us
    all_to_all x1, local copies, waits for them, and re-layouts, on_device(): lax.all_to_all(spectrum, 'fft', split_axis=2, concat_axis=1, tiled=True)  21.1 us
  transfers between devices with their start and end apart: 3, of which 3 were waited for; matrix products, arithmetic and copies ran while one was open for 1% of the time, Pallas kernels for 0%

commit v1 on v0

v1 whole, which is shorter than its diff:
```python
import functools
import math

import jax
import jax.numpy as jnp
import ml_dtypes
import numpy as np
from jax import lax
from jax.experimental import pallas as pl
from jax.experimental.pallas import tpu as pltpu
from jax.sharding import PartitionSpec as P

MESH = pl.DeviceIdType.MESH
N = 256
PLANES = 16
HALF = 129
BANDS = 8
GROUP = 16
PARTS = 4
W = 128

STEPS = (
    (2, 1, 0), (1, 0, 0), (3, 0, 1), (0, 1, 0), (2, 0, 0), (1, 1, 1), (3, 1, 0), (0, 1, 1),
    (2, 1, 1), (3, 0, 0), (1, 0, 1), (0, 0, 1), (2, 0, 1), (3, 1, 1), (1, 1, 0),
)


def cas_tables():
    steps = np.arange(N)
    angles = (steps[:, None] * steps[None, :] % N) * (2.0 * math.pi / N)
    table = np.cos(angles) + np.sin(angles)
    terms = []
    for _ in range(3):
        terms.append(table.astype(ml_dtypes.bfloat16))
        table = table - terms[-1].astype(np.float64)
    order = [terms[i] for i in (0, 1, 0, 1, 2, 0)]
    return np.concatenate(order, axis=0), np.concatenate(order, axis=1)


def split(x, axis, passes):
    high = x.astype(jnp.bfloat16)
    rest = x - high.astype(jnp.float32)
    middle = rest.astype(jnp.bfloat16)
    terms = [high, high, middle]
    if passes == 6:
        low = (rest - middle.astype(jnp.float32)).astype(jnp.bfloat16)
        terms = terms + [middle, high, low]
    return jnp.concatenate(terms, axis=axis)


def kernel(
    orb_hbm, flags, reach, tall, wide, out_hbm, margin,
    orb, fol, a0, a1, s0, s1, b0, b1, hin, acc, ktab, part, parts, fol_pass, hand_pass,
    load_sem, fol_send, fol_recv, fwd_send, fwd_recv, back_send, back_recv,
    hand_send, hand_recv, out_sem, sum_send, sum_recv, pass_send, pass_recv,
):
    band = lax.axis_index("band")
    me = lax.axis_index("fft")
    row = lax.rem(band, 4)
    across = 4 - 4 * (band // 4)
    after = lax.rem(band + 1, BANDS)
    before = lax.rem(band + BANDS - 1, BANDS)

    def partner(step):
        x, z, core = me // 4, (me // 2) % 2, me % 2
        return ((x + step[0]) % 4) * 4 + ((z + step[1]) % 2) * 2 + (core + step[2]) % 2

    def send(source, target, send_sem, recv_sem, device):
        pltpu.make_async_remote_copy(
            src_ref=source, dst_ref=target, send_sem=send_sem, recv_sem=recv_sem,
            device_id=device, device_id_type=MESH,
        ).start()

    def await_bytes(ref, sem):
        pltpu.make_async_copy(ref, ref, sem).wait()

    def right(x, passes):
        return jnp.dot(split(x, 1, passes), tall[: passes * N], preferred_element_type=jnp.float32)

    def left(x, passes):
        return jnp.dot(wide[:, : passes * N], split(x, 0, passes), preferred_element_type=jnp.float32)

    def put(ref, index, x):
        for h in range(2):
            ref[h, index] = x[:, h * W:(h + 1) * W]

    def line(ref, index):
        halves = [ref.at[h].reshape(N * PLANES, W)[pl.ds(index, N, stride=PLANES), :] for h in range(2)]
        return jnp.concatenate(halves, axis=1)

    loads = [
        pltpu.make_async_copy(
            orb_hbm.at[0, pl.ds(c * PARTS, PARTS)], orb.at[pl.ds(c * PARTS, PARTS)], load_sem.at[c]
        )
        for c in range(PARTS)
    ]
    for load in loads:
        load.start()

    barrier = pltpu.get_barrier_semaphore()
    for step in STEPS:
        pl.semaphore_signal(barrier, inc=1, device_id=(band, partner(step)), device_id_type=MESH)
    for ahead in range(1, BANDS):
        other = lax.rem(band + ahead, BANDS)
        pl.semaphore_signal(barrier, inc=1, device_id=(other, me), device_id_type=MESH)
    pl.semaphore_wait(barrier, GROUP - 1 + BANDS - 1)

    own_weight = flags[band, 0].astype(jnp.float32)
    next_weight = flags[band, 1].astype(jnp.float32)

    for c in range(PARTS):
        loads[c].wait()

    @pl.when(row != 0)
    def _():
        for c in range(PARTS):
            rows = pl.ds(c * PARTS, PARTS)
            send(orb.at[rows], fol.at[rows], fol_send, fol_recv.at[c], (before, me))

    @pl.when(row == 0)
    def _():
        for c in range(PARTS):
            rows = pl.ds(c * PARTS, PARTS)
            if c == 3:
                send(orb.at[rows], fol.at[rows], fol_send, fol_recv.at[c], (across + 3, me))
            else:
                send(orb.at[rows], fol_pass, fol_send, pass_recv.at[0], (across + c, me))

    def pass_following():
        @pl.when(row != 3)
        def _():
            await_bytes(fol_pass, pass_recv.at[0])
            rows = pl.ds(row * PARTS, PARTS)
            send(fol_pass, fol.at[rows], pass_send.at[0], fol_recv.at[row], (band - row + 3, me))

    def forward(c, pair, weight, spectrum, lines, which):
        for q in range(PARTS):
            p = c * PARTS + q
            density = weight * orb[p] * pair[p]
            put(spectrum, p, left(right(density, 6), 6))
        rows = pl.ds(c * PARTS, PARTS)
        mine = pl.ds(me * PLANES + c * PARTS, PARTS)
        for step in STEPS:
            g = partner(step)
            send(
                spectrum.at[:, rows, pl.ds(pl.multiple_of(g * PLANES, PLANES), PLANES)],
                lines.at[:, mine], fwd_send.at[which], fwd_recv.at[which], (band, g),
            )
        pltpu.make_async_copy(
            spectrum.at[:, rows, pl.ds(pl.multiple_of(me * PLANES, PLANES), PLANES)],
            lines.at[:, mine], fwd_recv.at[which],
        ).start()

    def own_chunk(c, carry):
        forward(c, orb, own_weight, a0, s0, 0)
        return carry

    lax.fori_loop(0, PARTS, own_chunk, 0)

    def fold(shape, axis):
        k = lax.broadcasted_iota(jnp.int32, shape, axis)
        return jnp.minimum(k, N - k)

    level = lax.broadcasted_iota(jnp.int32, (N, N), 1)
    pick_x = (fold((N, N), 0) == level).astype(jnp.bfloat16)
    by_x = jnp.dot(pick_x, reach[...], preferred_element_type=jnp.float32).astype(jnp.bfloat16)

    def table_step(k, carry):
        ky = me * PLANES + k
        fold_y = jnp.minimum(ky, N - ky)
        pick_y = (lax.broadcasted_iota(jnp.int32, (N, N), 0) == fold_y).astype(jnp.bfloat16)
        limit = jnp.dot(by_x, pick_y, preferred_element_type=jnp.float32)
        fold_x, fold_z = fold((N, N), 0), fold((N, N), 1)
        squares = fold_x * fold_x + fold_z * fold_z + fold_y * fold_y
        kept = (fold_z.astype(jnp.float32) <= limit) & (squares > 0)
        value = (64.0 / N**3) / jnp.maximum(squares, 1).astype(jnp.float32)
        ktab[k] = jnp.where(kept, value, 0.0)
        return carry

    lax.fori_loop(0, PLANES, table_step, 0)

    def cross_chunk(c, carry):
        await_bytes(fol.at[pl.ds(0, PARTS)], fol_recv.at[c])
        forward(c, fol, next_weight, a1, s1, 1)
        return carry

    def middle(lines, restored, which):
        await_bytes(lines, fwd_recv.at[which])
        await_bytes(restored.at[:, pl.ds(0, GROUP - 1)], fwd_send.at[which])

        def one(k):
            put(restored, k, left(left(line(lines, k), 6) * ktab[k], 3))

        def pair(i, carry):
            one(2 * i)
            one(2 * i + 1)
            return carry

        lax.fori_loop(0, PLANES // 2, pair, 0)

    def send_back(restored, mixed, which, j):
        mine = pl.ds(pl.multiple_of(me * PLANES, PLANES), PLANES)
        half = pl.ds(8 * j, 8)
        for step in STEPS:
            g = partner(step)
            send(
                restored.at[:, :, pl.ds(pl.multiple_of(g * PLANES + 8 * j, 8), 8)],
                mixed.at[:, mine, half], back_send.at[which], back_recv.at[which, j], (band, g),
            )
        pltpu.make_async_copy(
            restored.at[:, :, pl.ds(pl.multiple_of(me * PLANES + 8 * j, 8), 8)],
            mixed.at[:, mine, half], back_recv.at[which, j],
        ).start()

    pass_following()
    lax.fori_loop(0, PARTS // 2, cross_chunk, 0)
    middle(s0, a0, 0)
    send_back(a0, b0, 0, 0)
    send_back(a0, b0, 0, 1)
    lax.fori_loop(PARTS // 2, PARTS, cross_chunk, 0)
    middle(s1, a1, 1)
    send_back(a1, b1, 1, 0)
    send_back(a1, b1, 1, 1)

    def potential(mixed, p):
        return right(left(line(mixed, p), 3), 3)

    def hand(j):
        @pl.when(row != 3)
        def _():
            for c in (2 * j, 2 * j + 1):
                rows = pl.ds(PARTS * PLANES * c, PARTS * PLANES)
                send(s0.at[:, rows], hin.at[:, rows], hand_send, hand_recv.at[c], (after, me))

        @pl.when(row == 3)
        def _():
            for c in (2 * j, 2 * j + 1):
                rows = pl.ds(PARTS * PLANES * c, PARTS * PLANES)
                if c == 0:
                    send(s0.at[:, rows], hin.at[:, rows], hand_send, hand_recv.at[c], (across, me))
                else:
                    send(s0.at[:, rows], hand_pass, hand_send, pass_recv.at[1], (across + c, me))

    def pass_handed():
        @pl.when(row != 0)
        def _():
            await_bytes(hand_pass, pass_recv.at[1])
            rows = pl.ds(PARTS * PLANES * row, PARTS * PLANES)
            send(hand_pass, hin.at[:, rows], pass_send.at[1], hand_recv.at[row], (band - row, me))

    for j in range(2):
        await_bytes(b1.at[:, :, pl.ds(8 * j, 8)], back_recv.at[1, j])

        def cross_out(i, carry, j=j):
            for q in range(2):
                p = 8 * j + 2 * i + q
                coulomb = potential(b1, p)
                acc[p] = fol[p] * coulomb
                handed = orb[p] * coulomb
                for h in range(2):
                    s0[h, pl.ds(p * PLANES, PLANES)] = handed[:, h * W:(h + 1) * W].reshape(PLANES, PLANES, W)
            return carry

        lax.fori_loop(0, 4, cross_out, 0)
        hand(j)

    for j in range(2):
        await_bytes(b0.at[:, :, pl.ds(8 * j, 8)], back_recv.at[0, j])

        def own_out(i, carry, j=j):
            for q in range(2):
                p = 8 * j + 2 * i + q
                acc[p] = acc[p] + orb[p] * potential(b0, p)
            return carry

        lax.fori_loop(0, 4, own_out, 0)

    pass_handed()

    part[...] = jnp.zeros_like(part)
    for c in range(PARTS):
        await_bytes(hin.at[:, pl.ds(0, PARTS * PLANES)], hand_recv.at[c])

        def finish(i, carry, c=c):
            p = PARTS * c + i
            given = [hin[h, pl.ds(p * PLANES, PLANES)].reshape(N, W) for h in range(2)]
            field = -(acc[p] + jnp.concatenate(given, axis=1))
            acc[p] = field
            sums = (orb[p] * field).reshape(N // 8, 8, N).sum(axis=0)
            part[...] += sums[:, :W] + sums[:, W:]
            return carry

        lax.fori_loop(0, PARTS, finish, 0)
        rows = pl.ds(PARTS * c, PARTS)
        pltpu.make_async_copy(acc.at[rows], out_hbm.at[0, rows], out_sem.at[c]).start()

    for step in STEPS:
        send(part, parts.at[me], sum_send, sum_recv, (band, partner(step)))
    pltpu.make_async_copy(part, parts.at[me], sum_recv).start()
    await_bytes(parts, sum_recv)
    total = jnp.sum(jnp.sum(parts[...], axis=0), keepdims=True)
    margin[...] = total / float(N * N)

    await_bytes(parts.at[pl.ds(0, GROUP - 1)], sum_send)
    await_bytes(fol, fol_send)
    await_bytes(hin, hand_send)
    for which, restored in enumerate((a0, a1)):
        await_bytes(restored.at[:, pl.ds(0, GROUP - 1)], back_send.at[which])
    for c in range(PARTS):
        await_bytes(acc.at[pl.ds(PARTS * c, PARTS)], out_sem.at[c])

    @pl.when(row != 3)
    def _():
        await_bytes(fol_pass, pass_send.at[0])

    @pl.when(row != 0)
    def _():
        await_bytes(hand_pass, pass_send.at[1])


def on_device(orbitals, pair_flags, cutoff_reach):
    tall, wide = cas_tables()
    reach = jnp.pad(cutoff_reach.astype(jnp.bfloat16), ((0, N - HALF), (0, N - HALF)))
    block = pltpu.VMEM((PLANES, N, N), jnp.float32)
    planes = pltpu.VMEM((2, PLANES, N, W), jnp.float32)
    lines = pltpu.VMEM((2, N, PLANES, W), jnp.float32)
    dma = pltpu.SemaphoreType.DMA
    vmem = pl.BlockSpec(memory_space=pltpu.VMEM)
    anywhere = pl.BlockSpec(memory_space=pl.ANY)
    return pl.pallas_call(
        kernel,
        out_shape=(
            jax.ShapeDtypeStruct((1, PLANES, N, N), jnp.float32),
            jax.ShapeDtypeStruct((1, 1), jnp.float32),
        ),
        in_specs=[anywhere, pl.BlockSpec(memory_space=pltpu.SMEM), vmem, vmem, vmem],
        out_specs=(anywhere, vmem),
        scratch_shapes=[
            block, block, planes, planes, lines, lines, lines, lines, lines, block, block,
            pltpu.VMEM((8, 128), jnp.float32), pltpu.VMEM((GROUP, 8, 128), jnp.float32),
            pltpu.VMEM((PARTS, N, N), jnp.float32), pltpu.VMEM((2, PARTS * PLANES, PLANES, W), jnp.float32),
            dma((PARTS,)), dma, dma((PARTS,)), dma((2,)), dma((2,)), dma((2,)), dma((2, 2)),
            dma, dma((PARTS,)), dma((PARTS,)), dma, dma, dma((2,)), dma((2,)),
        ],
        compiler_params=pltpu.CompilerParams(
            collective_id=0, has_side_effects=True, vmem_limit_bytes=58 * 2**20
        ),
        name="exchange",
    )(orbitals, pair_flags, reach, jnp.asarray(tall), jnp.asarray(wide))


def solution(mesh):
    return jax.shard_map(
        on_device,
        mesh=mesh,
        in_specs=(P("band", "fft", None, None), P(), P()),
        out_specs=(P("band", "fft", None, None), P("band", None)),
        check_vma=False,
    )
```

time: 687 us -> 370 us (0.54); the launches traced: 677 us -> 369 us
  Pallas kernels: 0 us -> 359 us
  waiting for transfers between devices: 288 us -> 0 us
  blocking collectives: 184 us -> 0 us
  matrix products: 98.7 us -> 0 us
  local copies, waits for them, and re-layouts: 65.8 us -> 6.61 us
  other arithmetic: 23.6 us -> 0.92 us
  starting transfers between devices: 14.3 us -> 0 us
    pallas_call x0 -> x1, Pallas kernels: none -> 359 us  [on_device(): pl.pallas_call(kernel, out_shape=(jax.ShapeDtypeStruct((1, PLANES, N, N),...]
    all_to_all x1 -> x0, waiting for transfers between devices: 196 us -> none  [on_device(): lax.all_to_all(spectrum, 'fft', split_axis=2, concat_axis=1, tiled=True)]
    all_to_all x1 -> x0, blocking collectives: 149 us -> none  [on_device(): lax.all_to_all(restored, 'fft', split_axis=1, concat_axis=2, tiled=True)]
    dot_general x8 -> x0, matrix products: 98.7 us -> none  [the longest x2 30.3 us: transform_inner(): jnp.einsum('pxyz,zk->pxyk', densities, cas_table, precision=highest)]
    ppermute x2 -> x0, waiting for transfers between devices: 92.2 us -> none  [from_behind(): return lax.ppermute(block, axis, route)]
    psum x1 -> x0, blocking collectives: 34.5 us -> none  [on_device(): margin = lax.psum(local_margin, 'fft') / float(grid_size * grid_size)]
    transpose x2 -> x0, local copies, waits for them, and re-layouts: 32.7 us -> none  [the longest x1 16.4 us: on_device(): restored = jnp.einsum('pxyz,xk->pkyz', scaled, cas_table, precision=highest)]
    all_to_all x2 -> x0, local copies, waits for them, and re-layouts: 32.5 us -> none  [the longest x1 21.1 us: on_device(): lax.all_to_all(spectrum, 'fft', split_axis=2, concat_axis=1, tiled=True)]
  transfers between devices with their start and end apart: 3 -> 0, of which waited for: 3 -> 0; matrix products, arithmetic and copies ran while one was open for 1% -> 0% of each run, Pallas kernels for 0% -> 0%
where the time goes in v1:
time: 370 us; the launch traced here: 369 us
  Pallas kernels  359 us (97%)
  local copies, waits for them, and re-layouts  6.61 us (2%)
    pallas_call x1, Pallas kernels, on_device(): pl.pallas_call(kernel, out_shape=(jax.ShapeDtypeStruct((1, PLANES, N, N),...  359 us

profile of v1, /device:TPU:1, one launch (start us, length us, event | category | flops | bytes accessed | tf_op | source)
XLA Modules:
  0.0 369.4 jit_solution(18041805064520549720)
XLA Ops:
  0.6 1.3 copy.7.flags
  2.0 0.9 convert_element_type.5
  2.9 0.7 pad.4.reach
  3.6 359.5 %exchange.1 = (f32[1,16,256,256]{3,2,1,0:T(8,128)}, f32[1,1]{1,0:T(1,128)}) custom-call(f32[1,16,256,256]{3,2,1,0:T(8,128)} %orb_hbm.1, s32[8,2]{1,0:T(8,128)} %copy.7.flags, bf16[256,256]{1,0:T(8,128)(2,1)} %pad.4.reach, bf16[1536,256]{1,0:T(8,128)(2,1)} %constant.7.clone.tall, bf16[256,1536]{1,0:T(8,128)(2,1)} %constant.8.clone.wide), custom_call_target="tpu_custom_call" | custom-call | tf_op jit(solution)/shard_map/exchange/pallas_call | solution.py:330
  363.0 4.6 %copy.10 = f32[1,16,256,256]{3,2,1,0:T(8,128)} copy(f32[1,16,256,256]{3,2,1,0:T(8,128)} %get-tuple-element.4) | data formatting | bytes 8388608

commit v2 on v1

--- a/solution.py
+++ b/solution.py
@@ -18,6 +18,10 @@
 GROUP = 16
 PARTS = 4
 W = 128
+
+FOLLOWING = ((0, 4, 0), (4, 1, 0), (5, 3, 2), (8, 2, 2), (10, 2, None), (12, 4, None))
+NF = len(FOLLOWING)
+HANDED = (1, 3, 1, None)
 
 STEPS = (
     (2, 1, 0), (1, 0, 0), (3, 0, 1), (0, 1, 0), (2, 0, 0), (1, 1, 1), (3, 1, 0), (0, 1, 1),
@@ -49,11 +53,13 @@
 
 
 def kernel(
-    orb_hbm, flags, reach, tall, wide, out_hbm, margin,
-    orb, fol, a0, a1, s0, s1, b0, b1, hin, acc, ktab, part, parts, fol_pass, hand_pass,
-    load_sem, fol_send, fol_recv, fwd_send, fwd_recv, back_send, back_recv,
-    hand_send, hand_recv, out_sem, sum_send, sum_recv, pass_send, pass_recv,
+    orb_hbm, flags_hbm, reach_hbm, tall, wide, out, margin,
+    flags, reach, padded,
+    orb, fol, a0, a1, s0, s1, b0, b1, hin, ktab, part, parts, fol_pass, hand_pass,
+    small_sem, load_sem, fol_send, fol_recv, fwd_send, fwd_recv, back_send, back_recv,
+    hand_send, hand_recv, sum_send, sum_recv, pass_send, pass_recv,
 ):
+    acc = out.at[0]
     band = lax.axis_index("band")
     me = lax.axis_index("fft")
     row = lax.rem(band, 4)
@@ -94,7 +100,9 @@
         )
         for c in range(PARTS)
     ]
-    for load in loads:
+    flags_load = pltpu.make_async_copy(flags_hbm, flags, small_sem.at[0])
+    reach_load = pltpu.make_async_copy(reach_hbm, reach, small_sem.at[1])
+    for load in (*loads, flags_load, reach_load):
         load.start()
 
     barrier = pltpu.get_barrier_semaphore()
@@ -105,8 +113,9 @@
         pl.semaphore_signal(barrier, inc=1, device_id=(other, me), device_id_type=MESH)
     pl.semaphore_wait(barrier, GROUP - 1 + BANDS - 1)
 
-    own_weight = flags[band, 0].astype(jnp.float32)
-    next_weight = flags[band, 1].astype(jnp.float32)
+    flags_load.wait()
+    own_weight = flags[0, band].astype(jnp.float32)
+    next_weight = flags[1, band].astype(jnp.float32)
 
     for c in range(PARTS):
         loads[c].wait()
@@ -119,19 +128,22 @@
 
     @pl.when(row == 0)
     def _():
-        for c in range(PARTS):
-            rows = pl.ds(c * PARTS, PARTS)
-            if c == 3:
-                send(orb.at[rows], fol.at[rows], fol_send, fol_recv.at[c], (across + 3, me))
+        for n, (first, count, via) in enumerate(FOLLOWING):
+            rows = pl.ds(first, count)
+            if via is None:
+                send(orb.at[rows], fol.at[rows], fol_send, fol_recv.at[first // PARTS], (across + 3, me))
             else:
-                send(orb.at[rows], fol_pass, fol_send, pass_recv.at[0], (across + c, me))
+                send(orb.at[rows], fol_pass.at[rows], fol_send, pass_recv.at[n], (across + via, me))
 
     def pass_following():
-        @pl.when(row != 3)
-        def _():
-            await_bytes(fol_pass, pass_recv.at[0])
-            rows = pl.ds(row * PARTS, PARTS)
-            send(fol_pass, fol.at[rows], pass_send.at[0], fol_recv.at[row], (band - row + 3, me))
+        for n, (first, count, via) in enumerate(FOLLOWING):
+            if via is None:
+                continue
+
+            @pl.when(row == via)
+            def _(n=n, rows=pl.ds(first, count), via=via, c=first // PARTS):
+                await_bytes(fol_pass.at[rows], pass_recv.at[n])
+                send(fol_pass.at[rows], fol.at[rows], pass_send.at[n], fol_recv.at[c], (band - via + 3, me))
 
     def forward(c, pair, weight, spectrum, lines, which):
         for q in range(PARTS):
@@ -155,7 +167,7 @@
         forward(c, orb, own_weight, a0, s0, 0)
         return carry
 
-    lax.fori_loop(0, PARTS, own_chunk, 0)
+    lax.fori_loop(0, 2, own_chunk, 0)
 
     def fold(shape, axis):
         k = lax.broadcasted_iota(jnp.int32, shape, axis)
@@ -163,7 +175,11 @@
 
     level = lax.broadcasted_iota(jnp.int32, (N, N), 1)
     pick_x = (fold((N, N), 0) == level).astype(jnp.bfloat16)
-    by_x = jnp.dot(pick_x, reach[...], preferred_element_type=jnp.float32).astype(jnp.bfloat16)
+    reach_load.wait()
+    padded[...] = jnp.zeros_like(padded)
+    padded[:HALF, :HALF] = reach[...].astype(jnp.float32)
+    limits = padded[...].astype(jnp.bfloat16)
+    by_x = jnp.dot(pick_x, limits, preferred_element_type=jnp.float32).astype(jnp.bfloat16)
 
     def table_step(k, carry):
         ky = me * PLANES + k
@@ -179,48 +195,51 @@
 
     lax.fori_loop(0, PLANES, table_step, 0)
 
-    def cross_chunk(c, carry):
+    def cross_chunk(i, carry):
+        c = lax.rem(i + 3 * (row // 3), PARTS)
         await_bytes(fol.at[pl.ds(0, PARTS)], fol_recv.at[c])
         forward(c, fol, next_weight, a1, s1, 1)
         return carry
 
-    def middle(lines, restored, which):
+    def middle(lines, restored, which, mixed=None):
         await_bytes(lines, fwd_recv.at[which])
         await_bytes(restored.at[:, pl.ds(0, GROUP - 1)], fwd_send.at[which])
 
         def one(k):
             put(restored, k, left(left(line(lines, k), 6) * ktab[k], 3))
 
-        def pair(i, carry):
-            one(2 * i)
-            one(2 * i + 1)
+        def some(i, carry):
+            for k in range(PARTS):
+                one(PARTS * i + k)
+            if mixed is not None:
+                send_back(restored, mixed, which, 0, PARTS * i, PARTS)
             return carry
 
-        lax.fori_loop(0, PLANES // 2, pair, 0)
-
-    def send_back(restored, mixed, which, j):
-        mine = pl.ds(pl.multiple_of(me * PLANES, PLANES), PLANES)
+        lax.fori_loop(0, PLANES // PARTS, some, 0)
+
+    def send_back(restored, mixed, which, j, first=0, count=PLANES):
+        lines = pl.ds(first, count)
+        mine = pl.ds(me * PLANES + first, count)
         half = pl.ds(8 * j, 8)
         for step in STEPS:
             g = partner(step)
             send(
-                restored.at[:, :, pl.ds(pl.multiple_of(g * PLANES + 8 * j, 8), 8)],
+                restored.at[:, lines, pl.ds(pl.multiple_of(g * PLANES + 8 * j, 8), 8)],
                 mixed.at[:, mine, half], back_send.at[which], back_recv.at[which, j], (band, g),
             )
         pltpu.make_async_copy(
-            restored.at[:, :, pl.ds(pl.multiple_of(me * PLANES + 8 * j, 8), 8)],
+            restored.at[:, lines, pl.ds(pl.multiple_of(me * PLANES + 8 * j, 8), 8)],
             mixed.at[:, mine, half], back_recv.at[which, j],
         ).start()
 
     pass_following()
-    lax.fori_loop(0, PARTS // 2, cross_chunk, 0)
+    lax.fori_loop(0, 2, cross_chunk, 0)
+    lax.fori_loop(2, 3, own_chunk, 0)
+    lax.fori_loop(2, 4, cross_chunk, 0)
+    lax.fori_loop(3, 4, own_chunk, 0)
+    middle(s1, a1, 1, b1)
+    send_back(a1, b1, 1, 1)
     middle(s0, a0, 0)
-    send_back(a0, b0, 0, 0)
-    send_back(a0, b0, 0, 1)
-    lax.fori_loop(PARTS // 2, PARTS, cross_chunk, 0)
-    middle(s1, a1, 1)
-    send_back(a1, b1, 1, 0)
-    send_back(a1, b1, 1, 1)
 
     def potential(mixed, p):
         return right(left(line(mixed, p), 3), 3)
@@ -236,17 +255,21 @@
         def _():
             for c in (2 * j, 2 * j + 1):
                 rows = pl.ds(PARTS * PLANES * c, PARTS * PLANES)
-                if c == 0:
+                via = HANDED[c]
+                if via is None:
                     send(s0.at[:, rows], hin.at[:, rows], hand_send, hand_recv.at[c], (across, me))
                 else:
-                    send(s0.at[:, rows], hand_pass, hand_send, pass_recv.at[1], (across + c, me))
+                    send(s0.at[:, rows], hand_pass.at[:, rows], hand_send, pass_recv.at[NF + c], (across + via, me))
 
     def pass_handed():
-        @pl.when(row != 0)
-        def _():
-            await_bytes(hand_pass, pass_recv.at[1])
-            rows = pl.ds(PARTS * PLANES * row, PARTS * PLANES)
-            send(hand_pass, hin.at[:, rows], pass_send.at[1], hand_recv.at[row], (band - row, me))
+        for c, via in enumerate(HANDED):
+            if via is None:
+                continue
+
+            @pl.when(row == via)
+            def _(c=c, rows=pl.ds(PARTS * PLANES * c, PARTS * PLANES), via=via):
+                await_bytes(hand_pass.at[:, rows], pass_recv.at[NF + c])
+                send(hand_pass.at[:, rows], hin.at[:, rows], pass_send.at[NF + c], hand_recv.at[c], (band - via, me))
 
     for j in range(2):
         await_bytes(b1.at[:, :, pl.ds(8 * j, 8)], back_recv.at[1, j])
@@ -263,6 +286,9 @@
 
         lax.fori_loop(0, 4, cross_out, 0)
         hand(j)
+        send_back(a0, b0, 0, j)
+
+    pass_handed()
 
     for j in range(2):
         await_bytes(b0.at[:, :, pl.ds(8 * j, 8)], back_recv.at[0, j])
@@ -274,8 +300,6 @@
             return carry
 
         lax.fori_loop(0, 4, own_out, 0)
-
-    pass_handed()
 
     part[...] = jnp.zeros_like(part)
     for c in range(PARTS):
@@ -291,8 +315,6 @@
             return carry
 
         lax.fori_loop(0, PARTS, finish, 0)
-        rows = pl.ds(PARTS * c, PARTS)
-        pltpu.make_async_copy(acc.at[rows], out_hbm.at[0, rows], out_sem.at[c]).start()
 
     for step in STEPS:
         send(part, parts.at[me], sum_send, sum_recv, (band, partner(step)))
@@ -306,21 +328,23 @@
     await_bytes(hin, hand_send)
     for which, restored in enumerate((a0, a1)):
         await_bytes(restored.at[:, pl.ds(0, GROUP - 1)], back_send.at[which])
-    for c in range(PARTS):
-        await_bytes(acc.at[pl.ds(PARTS * c, PARTS)], out_sem.at[c])
-
-    @pl.when(row != 3)
-    def _():
-        await_bytes(fol_pass, pass_send.at[0])
-
-    @pl.when(row != 0)
-    def _():
-        await_bytes(hand_pass, pass_send.at[1])
+    for n, (first, count, via) in enumerate(FOLLOWING):
+        if via is not None:
+
+            @pl.when(row == via)
+            def _(n=n, rows=pl.ds(first, count)):
+                await_bytes(fol_pass.at[rows], pass_send.at[n])
+
+    for c, via in enumerate(HANDED):
+        if via is not None:
+
+            @pl.when(row == via)
+            def _(c=c, rows=pl.ds(PARTS * PLANES * c, PARTS * PLANES)):
+                await_bytes(hand_pass.at[:, rows], pass_send.at[NF + c])
 
 
 def on_device(orbitals, pair_flags, cutoff_reach):
     tall, wide = cas_tables()
-    reach = jnp.pad(cutoff_reach.astype(jnp.bfloat16), ((0, N - HALF), (0, N - HALF)))
     block = pltpu.VMEM((PLANES, N, N), jnp.float32)
     planes = pltpu.VMEM((2, PLANES, N, W), jnp.float32)
     lines = pltpu.VMEM((2, N, PLANES, W), jnp.float32)
@@ -330,23 +354,24 @@
     return pl.pallas_call(
         kernel,
         out_shape=(
-            jax.ShapeDtypeStruct((1, PLANES, N, N), jnp.float32),
+            pltpu.VMEM((1, PLANES, N, N), jnp.float32),
             jax.ShapeDtypeStruct((1, 1), jnp.float32),
         ),
-        in_specs=[anywhere, pl.BlockSpec(memory_space=pltpu.SMEM), vmem, vmem, vmem],
-        out_specs=(anywhere, vmem),
+        in_specs=[anywhere, anywhere, anywhere, vmem, vmem],
+        out_specs=(vmem, vmem),
         scratch_shapes=[
-            block, block, planes, planes, lines, lines, lines, lines, lines, block, block,
+            pltpu.SMEM((2, BANDS), jnp.int32), pltpu.VMEM((HALF, HALF), jnp.int32), pltpu.VMEM((N, N), jnp.float32),
+            block, block, planes, planes, lines, lines, lines, lines, lines, block,
             pltpu.VMEM((8, 128), jnp.float32), pltpu.VMEM((GROUP, 8, 128), jnp.float32),
-            pltpu.VMEM((PARTS, N, N), jnp.float32), pltpu.VMEM((2, PARTS * PLANES, PLANES, W), jnp.float32),
-            dma((PARTS,)), dma, dma((PARTS,)), dma((2,)), dma((2,)), dma((2,)), dma((2, 2)),
-            dma, dma((PARTS,)), dma((PARTS,)), dma, dma, dma((2,)), dma((2,)),
+            pltpu.VMEM((10, N, N), jnp.float32), lines,
+            dma((2,)), dma((PARTS,)), dma, dma((PARTS,)), dma((2,)), dma((2,)), dma((2,)), dma((2, 2)),
+            dma, dma((PARTS,)), dma, dma, dma((NF + PARTS,)), dma((NF + PARTS,)),
         ],
         compiler_params=pltpu.CompilerParams(
-            collective_id=0, has_side_effects=True, vmem_limit_bytes=58 * 2**20
+            collective_id=0, has_side_effects=True, vmem_limit_bytes=54 * 2**20
         ),
         name="exchange",
-    )(orbitals, pair_flags, reach, jnp.asarray(tall), jnp.asarray(wide))
+    )(orbitals, pair_flags.T, cutoff_reach, jnp.asarray(tall), jnp.asarray(wide))
 
 
 def solution(mesh):

time: 370 us -> 288 us (0.78)
  Pallas kernels: 359 us -> 284 us
  local copies, waits for them, and re-layouts: 6.61 us -> 2.02 us
    pallas_call x1, Pallas kernels: 359 us -> 284 us  [on_device(): pl.pallas_call(kernel, out_shape=(pltpu.VMEM((1, PLANES, N, N), jnp.float...]
    unnamed x2 -> x1, local copies, waits for them, and re-layouts: 5.94 us -> 2.02 us
where the time goes in v2:
time: 288 us
  Pallas kernels  284 us (99%)
    pallas_call x1, Pallas kernels, on_device(): pl.pallas_call(kernel, out_shape=(pltpu.VMEM((1, PLANES, N, N), jnp.float...  284 us

profile of v2, /device:TPU:1, one launch (start us, length us, event | category | flops | bytes accessed | tf_op | source)
XLA Modules:
  0.0 287.9 jit_solution(10008505024652786652)
XLA Ops:
  0.6 283.6 %exchange.1 = (f32[1,16,256,256]{3,2,1,0:T(8,128)S(1)}, f32[1,1]{1,0:T(1,128)}) custom-call(f32[1,16,256,256]{3,2,1,0:T(8,128)} %orb_hbm.1, s32[2,8]{1,0:T(2,128)} %bitcast.1, s32[129,129]{1,0:T(8,128)} %reach_hbm.1, bf16[1536,256]{1,0:T(8,128)(2,1)} %constant.4.clone.tall, bf16[256,1536]{1,0:T(8,128)(2,1)} %constant.5.clone.wide), custom_call_target="tpu_custom_call" | custom-call | tf_op jit(solution)/shard_map/exchange/pallas_call | solution.py:354
  284.2 2.0 copy.9

commit v3 on v2

--- a/solution.py
+++ b/solution.py
@@ -167,7 +167,7 @@
         forward(c, orb, own_weight, a0, s0, 0)
         return carry
 
-    lax.fori_loop(0, 2, own_chunk, 0)
+    own_chunk(0, 0)
 
     def fold(shape, axis):
         k = lax.broadcasted_iota(jnp.int32, shape, axis)
@@ -217,24 +217,32 @@
 
         lax.fori_loop(0, PLANES // PARTS, some, 0)
 
-    def send_back(restored, mixed, which, j, first=0, count=PLANES):
+    def send_back(restored, mixed, which, j, first=0, count=PLANES, z=None):
         lines = pl.ds(first, count)
         mine = pl.ds(me * PLANES + first, count)
         half = pl.ds(8 * j, 8)
         for step in STEPS:
+            if z is not None and step[1] != z:
+                continue
             g = partner(step)
             send(
                 restored.at[:, lines, pl.ds(pl.multiple_of(g * PLANES + 8 * j, 8), 8)],
                 mixed.at[:, mine, half], back_send.at[which], back_recv.at[which, j], (band, g),
             )
-        pltpu.make_async_copy(
-            restored.at[:, lines, pl.ds(pl.multiple_of(me * PLANES + 8 * j, 8), 8)],
-            mixed.at[:, mine, half], back_recv.at[which, j],
-        ).start()
+        if z != 1:
+            pltpu.make_async_copy(
+                restored.at[:, lines, pl.ds(pl.multiple_of(me * PLANES + 8 * j, 8), 8)],
+                mixed.at[:, mine, half], back_recv.at[which, j],
+            ).start()
 
     pass_following()
-    lax.fori_loop(0, 2, cross_chunk, 0)
-    lax.fori_loop(2, 3, own_chunk, 0)
+
+    def alternate(i, carry):
+        cross_chunk(i, carry)
+        own_chunk(i + 1, carry)
+        return carry
+
+    lax.fori_loop(0, 2, alternate, 0)
     lax.fori_loop(2, 4, cross_chunk, 0)
     lax.fori_loop(3, 4, own_chunk, 0)
     middle(s1, a1, 1, b1)
@@ -261,8 +269,9 @@
                 else:
                     send(s0.at[:, rows], hand_pass.at[:, rows], hand_send, pass_recv.at[NF + c], (across + via, me))
 
-    def pass_handed():
-        for c, via in enumerate(HANDED):
+    def pass_handed(parts):
+        for c in parts:
+            via = HANDED[c]
             if via is None:
                 continue
 
@@ -286,9 +295,12 @@
 
         lax.fori_loop(0, 4, cross_out, 0)
         hand(j)
-        send_back(a0, b0, 0, j)
-
-    pass_handed()
+        send_back(a0, b0, 0, j, z=0)
+
+    pass_handed((0, 1))
+    send_back(a0, b0, 0, 0, z=1)
+    pass_handed((2, 3))
+    send_back(a0, b0, 0, 1, z=1)
 
     for j in range(2):
         await_bytes(b0.at[:, :, pl.ds(8 * j, 8)], back_recv.at[0, j])

time: 288 us -> 279 us (0.969)
  the two profiles are of different devices: /device:TPU:1 before, /device:TPU:8 now
where the time goes in v3:
time: 279 us
  Pallas kernels  274 us (98%)
    pallas_call x1, Pallas kernels, on_device(): pl.pallas_call(kernel, out_shape=(pltpu.VMEM((1, PLANES, N, N), jnp.float...  274 us

profile of v3, /device:TPU:8, one launch (start us, length us, event | category | flops | bytes accessed | tf_op | source)
XLA Modules:
  0.0 278.6 jit_solution(13310591204589858008)
XLA Ops:
  0.6 274.2 %exchange.1 = (f32[1,16,256,256]{3,2,1,0:T(8,128)S(1)}, f32[1,1]{1,0:T(1,128)}) custom-call(f32[1,16,256,256]{3,2,1,0:T(8,128)} %orb_hbm.1, s32[2,8]{1,0:T(2,128)} %bitcast.1, s32[129,129]{1,0:T(8,128)} %reach_hbm.1, bf16[1536,256]{1,0:T(8,128)(2,1)} %constant.4.clone.tall, bf16[256,1536]{1,0:T(8,128)(2,1)} %constant.5.clone.wide), custom_call_target="tpu_custom_call" | custom-call | tf_op jit(solution)/shard_map/exchange/pallas_call | solution.py:366
  274.8 2.0 copy.9

commit v4 on v3

--- a/solution.py
+++ b/solution.py
@@ -19,9 +19,9 @@
 PARTS = 4
 W = 128
 
-FOLLOWING = ((0, 4, 0), (4, 1, 0), (5, 3, 2), (8, 2, 2), (10, 2, None), (12, 4, None))
+FOLLOWING = ((0, 4, (0,)), (4, 1, (0,)), (5, 3, (2,)), (8, 2, (2,)), (10, 2, ()), (12, 4, ()))
+HANDED = ((0, 4, (1,)), (4, 4, (3,)), (8, 4, (1,)), (12, 4, ()))
 NF = len(FOLLOWING)
-HANDED = (1, 3, 1, None)
 
 STEPS = (
     (2, 1, 0), (1, 0, 0), (3, 0, 1), (0, 1, 0), (2, 0, 0), (1, 1, 1), (3, 1, 0), (0, 1, 1),
@@ -128,28 +128,39 @@
 
     @pl.when(row == 0)
     def _():
-        for n, (first, count, via) in enumerate(FOLLOWING):
+        for n, (first, count, path) in enumerate(FOLLOWING):
             rows = pl.ds(first, count)
-            if via is None:
+            if path:
+                send(orb.at[rows], fol_pass.at[rows], fol_send, pass_recv.at[n], (across + path[0], me))
+            else:
                 send(orb.at[rows], fol.at[rows], fol_send, fol_recv.at[first // PARTS], (across + 3, me))
+
+    def pass_on(n, held, rows, path, hop, final, arrived, end):
+        @pl.when(row == path[hop])
+        def _():
+            await_bytes(held(rows), pass_recv.at[n])
+            base = band - path[hop]
+            if hop + 1 < len(path):
+                send(held(rows), held(rows), pass_send.at[n], pass_recv.at[n], (base + path[hop + 1], me))
             else:
-                send(orb.at[rows], fol_pass.at[rows], fol_send, pass_recv.at[n], (across + via, me))
-
-    def pass_following():
-        for n, (first, count, via) in enumerate(FOLLOWING):
-            if via is None:
-                continue
-
-            @pl.when(row == via)
-            def _(n=n, rows=pl.ds(first, count), via=via, c=first // PARTS):
-                await_bytes(fol_pass.at[rows], pass_recv.at[n])
-                send(fol_pass.at[rows], fol.at[rows], pass_send.at[n], fol_recv.at[c], (band - via + 3, me))
+                send(held(rows), final(rows), pass_send.at[n], arrived, (base + end, me))
+
+    def pass_following(n, hop):
+        first, count, path = FOLLOWING[n]
+        pass_on(
+            n, lambda r: fol_pass.at[r], pl.ds(first, count), path, hop,
+            lambda r: fol.at[r], fol_recv.at[first // PARTS], 3,
+        )
 
     def forward(c, pair, weight, spectrum, lines, which):
-        for q in range(PARTS):
-            p = c * PARTS + q
-            density = weight * orb[p] * pair[p]
-            put(spectrum, p, left(right(density, 6), 6))
+        def some_planes(i, carry):
+            for q in range(2):
+                p = c * PARTS + 2 * i + q
+                density = weight * orb[p] * pair[p]
+                put(spectrum, p, left(right(density, 6), 6))
+            return carry
+
+        lax.fori_loop(0, PARTS // 2, some_planes, 0)
         rows = pl.ds(c * PARTS, PARTS)
         mine = pl.ds(me * PLANES + c * PARTS, PARTS)
         for step in STEPS:
@@ -195,11 +206,10 @@
 
     lax.fori_loop(0, PLANES, table_step, 0)
 
-    def cross_chunk(i, carry):
-        c = lax.rem(i + 3 * (row // 3), PARTS)
+    def cross_chunk(i, shift):
+        c = lax.rem(i + (row // 3) * shift, PARTS)
         await_bytes(fol.at[pl.ds(0, PARTS)], fol_recv.at[c])
         forward(c, fol, next_weight, a1, s1, 1)
-        return carry
 
     def middle(lines, restored, which, mixed=None):
         await_bytes(lines, fwd_recv.at[which])
@@ -209,8 +219,12 @@
             put(restored, k, left(left(line(lines, k), 6) * ktab[k], 3))
 
         def some(i, carry):
-            for k in range(PARTS):
-                one(PARTS * i + k)
+            def few(n, inner):
+                for q in range(2):
+                    one(PARTS * i + 2 * n + q)
+                return inner
+
+            lax.fori_loop(0, PARTS // 2, few, 0)
             if mixed is not None:
                 send_back(restored, mixed, which, 0, PARTS * i, PARTS)
             return carry
@@ -235,16 +249,20 @@
                 mixed.at[:, mine, half], back_recv.at[which, j],
             ).start()
 
-    pass_following()
-
-    def alternate(i, carry):
-        cross_chunk(i, carry)
-        own_chunk(i + 1, carry)
+    for n in range(4):
+        pass_following(n, 0)
+    cross_chunk(0, 3)
+    own_chunk(1, 0)
+    cross_chunk(1, 3)
+    early = jnp.where(row == 1, 1, 0)
+    lax.fori_loop(2, 3 + early, own_chunk, 0)
+
+    def last_two(i, carry):
+        cross_chunk(i, 3)
         return carry
 
-    lax.fori_loop(0, 2, alternate, 0)
-    lax.fori_loop(2, 4, cross_chunk, 0)
-    lax.fori_loop(3, 4, own_chunk, 0)
+    lax.fori_loop(2, 4, last_two, 0)
+    lax.fori_loop(3 + early, 4, own_chunk, 0)
     middle(s1, a1, 1, b1)
     send_back(a1, b1, 1, 1)
     middle(s0, a0, 0)
@@ -261,24 +279,22 @@
 
         @pl.when(row == 3)
         def _():
-            for c in (2 * j, 2 * j + 1):
-                rows = pl.ds(PARTS * PLANES * c, PARTS * PLANES)
-                via = HANDED[c]
-                if via is None:
-                    send(s0.at[:, rows], hin.at[:, rows], hand_send, hand_recv.at[c], (across, me))
+            for n, (first, count, path) in enumerate(HANDED):
+                if first // 8 != j:
+                    continue
+                rows = pl.ds(PLANES * first, PLANES * count)
+                if path:
+                    target, arrived, device = hand_pass, pass_recv.at[NF + n], across + path[0]
                 else:
-                    send(s0.at[:, rows], hand_pass.at[:, rows], hand_send, pass_recv.at[NF + c], (across + via, me))
-
-    def pass_handed(parts):
-        for c in parts:
-            via = HANDED[c]
-            if via is None:
-                continue
-
-            @pl.when(row == via)
-            def _(c=c, rows=pl.ds(PARTS * PLANES * c, PARTS * PLANES), via=via):
-                await_bytes(hand_pass.at[:, rows], pass_recv.at[NF + c])
-                send(hand_pass.at[:, rows], hin.at[:, rows], pass_send.at[NF + c], hand_recv.at[c], (band - via, me))
+                    target, arrived, device = hin, hand_recv.at[first // PARTS], across
+                send(s0.at[:, rows], target.at[:, rows], hand_send, arrived, (device, me))
+
+    def pass_handed(n, hop):
+        first, count, path = HANDED[n]
+        pass_on(
+            NF + n, lambda r: hand_pass.at[:, r], pl.ds(PLANES * first, PLANES * count), path, hop,
+            lambda r: hin.at[:, r], hand_recv.at[first // PARTS], 0,
+        )
 
     for j in range(2):
         await_bytes(b1.at[:, :, pl.ds(8 * j, 8)], back_recv.at[1, j])
@@ -297,9 +313,10 @@
         hand(j)
         send_back(a0, b0, 0, j, z=0)
 
-    pass_handed((0, 1))
+    pass_handed(0, 0)
+    pass_handed(1, 0)
     send_back(a0, b0, 0, 0, z=1)
-    pass_handed((2, 3))
+    pass_handed(2, 0)
     send_back(a0, b0, 0, 1, z=1)
 
     for j in range(2):
@@ -340,19 +357,19 @@
     await_bytes(hin, hand_send)
     for which, restored in enumerate((a0, a1)):
         await_bytes(restored.at[:, pl.ds(0, GROUP - 1)], back_send.at[which])
-    for n, (first, count, via) in enumerate(FOLLOWING):
-        if via is not None:
-
-            @pl.when(row == via)
+    for n, (first, count, path) in enumerate(FOLLOWING):
+        for at_row in path:
+
+            @pl.when(row == at_row)
             def _(n=n, rows=pl.ds(first, count)):
                 await_bytes(fol_pass.at[rows], pass_send.at[n])
 
-    for c, via in enumerate(HANDED):
-        if via is not None:
-
-            @pl.when(row == via)
-            def _(c=c, rows=pl.ds(PARTS * PLANES * c, PARTS * PLANES)):
-                await_bytes(hand_pass.at[:, rows], pass_send.at[NF + c])
+    for n, (first, count, path) in enumerate(HANDED):
+        for at_row in path:
+
+            @pl.when(row == at_row)
+            def _(n=n, rows=pl.ds(PLANES * first, PLANES * count)):
+                await_bytes(hand_pass.at[:, rows], pass_send.at[NF + n])
 
 
 def on_device(orbitals, pair_flags, cutoff_reach):
@@ -375,9 +392,9 @@
             pltpu.SMEM((2, BANDS), jnp.int32), pltpu.VMEM((HALF, HALF), jnp.int32), pltpu.VMEM((N, N), jnp.float32),
             block, block, planes, planes, lines, lines, lines, lines, lines, block,
             pltpu.VMEM((8, 128), jnp.float32), pltpu.VMEM((GROUP, 8, 128), jnp.float32),
-            pltpu.VMEM((10, N, N), jnp.float32), lines,
+            pltpu.VMEM((12, N, N), jnp.float32), lines,
             dma((2,)), dma((PARTS,)), dma, dma((PARTS,)), dma((2,)), dma((2,)), dma((2,)), dma((2, 2)),
-            dma, dma((PARTS,)), dma, dma, dma((NF + PARTS,)), dma((NF + PARTS,)),
+            dma, dma((PARTS,)), dma, dma, dma((NF + len(HANDED),)), dma((NF + len(HANDED),)),
         ],
         compiler_params=pltpu.CompilerParams(
             collective_id=0, has_side_effects=True, vmem_limit_bytes=54 * 2**20

time: 279 us -> 276 us (0.989)
  the two profiles are of different devices: /device:TPU:8 before, /device:TPU:1 now
where the time goes in v4:
time: 276 us; the launch traced here: 271 us
  Pallas kernels  266 us (96%)
    pallas_call x1, Pallas kernels, on_device(): pl.pallas_call(kernel, out_shape=(pltpu.VMEM((1, PLANES, N, N), jnp.float...  266 us

profile of v4, /device:TPU:1, one launch (start us, length us, event | category | flops | bytes accessed | tf_op | source)
XLA Modules:
  0.0 270.8 jit_solution(17772997055376151540)
XLA Ops:
  0.6 266.5 %exchange.1 = (f32[1,16,256,256]{3,2,1,0:T(8,128)S(1)}, f32[1,1]{1,0:T(1,128)}) custom-call(f32[1,16,256,256]{3,2,1,0:T(8,128)} %orb_hbm.1, s32[2,8]{1,0:T(2,128)} %bitcast.1, s32[129,129]{1,0:T(8,128)} %reach_hbm.1, bf16[1536,256]{1,0:T(8,128)(2,1)} %constant.4.clone.tall, bf16[256,1536]{1,0:T(8,128)(2,1)} %constant.5.clone.wide), custom_call_target="tpu_custom_call" | custom-call | tf_op jit(solution)/shard_map/exchange/pallas_call | solution.py:383
  267.1 2.0 copy.9

commit v5 on v4

--- a/solution.py
+++ b/solution.py
@@ -19,7 +19,7 @@
 PARTS = 4
 W = 128
 
-FOLLOWING = ((0, 4, (0,)), (4, 1, (0,)), (5, 3, (2,)), (8, 2, (2,)), (10, 2, ()), (12, 4, ()))
+FOLLOWING = ((0, 4, (0,)), (4, 4, (2,)), (8, 2, (2,)), (10, 2, ()), (12, 4, ()))
 HANDED = ((0, 4, (1,)), (4, 4, (3,)), (8, 4, (1,)), (12, 4, ()))
 NF = len(FOLLOWING)
 
@@ -249,7 +249,7 @@
                 mixed.at[:, mine, half], back_recv.at[which, j],
             ).start()
 
-    for n in range(4):
+    for n in range(3):
         pass_following(n, 0)
     cross_chunk(0, 3)
     own_chunk(1, 0)

time: 276 us -> 276 us (level); the launches traced: 271 us -> 276 us
  Pallas kernels: 266 us -> 272 us
    pallas_call x1, Pallas kernels: 266 us -> 272 us  [on_device(): pl.pallas_call(kernel, out_shape=(pltpu.VMEM((1, PLANES, N, N), jnp.float...]
where the time goes in v5:
time: 276 us
  Pallas kernels  272 us (99%)
    pallas_call x1, Pallas kernels, on_device(): pl.pallas_call(kernel, out_shape=(pltpu.VMEM((1, PLANES, N, N), jnp.float...  272 us

profile of v5, /device:TPU:1, one launch (start us, length us, event | category | flops | bytes accessed | tf_op | source)
XLA Modules:
  0.0 276.0 jit_solution(6365882347300323033)
XLA Ops:
  0.6 271.6 %exchange.1 = (f32[1,16,256,256]{3,2,1,0:T(8,128)S(1)}, f32[1,1]{1,0:T(1,128)}) custom-call(f32[1,16,256,256]{3,2,1,0:T(8,128)} %orb_hbm.1, s32[2,8]{1,0:T(2,128)} %bitcast.1, s32[129,129]{1,0:T(8,128)} %reach_hbm.1, bf16[1536,256]{1,0:T(8,128)(2,1)} %constant.4.clone.tall, bf16[256,1536]{1,0:T(8,128)(2,1)} %constant.5.clone.wide), custom_call_target="tpu_custom_call" | custom-call | tf_op jit(solution)/shard_map/exchange/pallas_call | solution.py:383
  272.3 2.0 copy.9
